TPU v7x, 128 devices: a whole 4x4x4 slice. The times are simulated.
128 devices in a mesh: dp: 16 (over x, z_lo, core), pipe: 8 (over y, z_hi).
Axes of the slice: x: 4, y: 4, z: 4 (z_hi: 2, z_lo: 2; z = z_hi * 2 + z_lo), core: 2. Of those that a mesh axis runs over, the one named last changes fastest.
Arguments:
- shallow: bfloat16 [4096, 8192], P('dp'), may hold values from -8 to 8
- teacher: bfloat16 [4096, 8192], P(('dp', 'pipe')), may hold values from -8 to 8
- positions: int32 [4096], P('dp'), may hold values from 0 to 4095
- segments: int32 [4096], P('dp'), may hold values from 0 to 255, never falling along the last dimension, each value on 1 to 64 neighbouring positions
- in_gain: float32 [8192], replicated, may hold values from 0.2 to 4.5
- w_query: bfloat16 [8192, 4096], P('dp', 'pipe'), may hold values from -0.0625 to 0.0625
- w_keyval: bfloat16 [8192, 1024], P('dp', 'pipe'), may hold values from -0.0625 to 0.0625
- w_output: bfloat16 [4096, 8192], P('pipe', 'dp'), may hold values from -0.09375 to 0.09375
Outputs:
- loss: float32 [], replicated
- step_query: float32 [8192, 4096], P('dp', 'pipe')
- step_keyval: float32 [8192, 1024], P('dp', 'pipe')
- step_output: float32 [4096, 8192], P('pipe', 'dp')
Inputs may be any that keep to these rules, and one draw needn't show every extreme that they name: `segments`: ids never fall along the rows; every segment covers 1 to 64 rows.
All inputs are finite; a program needn't handle non-finite values.
Results may differ from a plain program's by a relative error of at most 0.023.
Values may be sent and summed in bfloat16 or wider, within the bound.
A program may use at most 128 MiB of HBM per device.

v0:
```python
import math
import jax
import jax.numpy as jnp
from jax import lax
from jax.sharding import PartitionSpec as P

D = 8192
HD = 128
QH = 32
KV = 4
theta_base = 10000.0
norm_eps = 1e-05
cosine_eps = 1e-06
mean_eps = 1e-12
mask_fill = -1e30


def shifted(value, axis, steps):
    count = lax.axis_size(axis)
    pairs = [(source, (source + steps) % count) for source in range(count)]
    return lax.ppermute(value, axis, pairs)


def normalize_rows(rows_in, in_gain):
    widened = rows_in.astype(jnp.float32)
    spread = jnp.mean(widened * widened, axis=-1, keepdims=True)
    return (widened * lax.rsqrt(spread + norm_eps) * in_gain[None, :]).astype(jnp.bfloat16)


def rotary_tables(positions, head_width):
    half_width = head_width // 2
    exponent = jnp.arange(half_width).astype(jnp.float32) * (2.0 / head_width)
    inverse = jnp.power(jnp.float32(theta_base), -exponent)
    angle_table = positions.astype(jnp.float32)[:, None] * inverse[None, :]
    return (jnp.cos(angle_table), jnp.sin(angle_table))


def rotate(values, cosine, sine_table):
    half_width = values.shape[-1] // 2
    leading = values[..., :half_width]
    trailing = values[..., half_width:]
    cosine_row = cosine[:, None, :]
    sine_row = sine_table[:, None, :]
    return jnp.concatenate(
        [leading * cosine_row - trailing * sine_row, trailing * cosine_row + leading * sine_row],
        axis=-1,
    )


def unrotate(values, cosine, sine_table):
    half_width = values.shape[-1] // 2
    leading = values[..., :half_width]
    trailing = values[..., half_width:]
    cosine_row = cosine[:, None, :]
    sine_row = sine_table[:, None, :]
    return jnp.concatenate(
        [leading * cosine_row + trailing * sine_row, trailing * cosine_row - leading * sine_row],
        axis=-1,
    )


def attend(queries, keys_head, values_head, allowed):
    score_scale = 1.0 / math.sqrt(queries.shape[-1])
    scores = (
        jnp.einsum("rhd,khd->hrk", queries, keys_head, preferred_element_type=jnp.float32)
        * score_scale
    )
    scores = jnp.where(allowed[None], scores, mask_fill)
    highest = jnp.max(scores, axis=-1, keepdims=True)
    weights = jnp.exp(scores - highest)
    softmax_rows = weights / jnp.sum(weights, axis=-1, keepdims=True)
    softmax_low = softmax_rows.astype(jnp.bfloat16)
    attended = jnp.einsum(
        "hrk,khd->rhd", softmax_low, values_head, preferred_element_type=jnp.float32
    ).astype(jnp.bfloat16)
    return (softmax_rows, softmax_low, attended)


def attend_grad(softmax_rows, softmax_low, queries, keys_head, values_head, att_grad):
    score_scale = 1.0 / math.sqrt(queries.shape[-1])
    inner_prod = jnp.einsum(
        "rhd,khd->hrk", att_grad, values_head, preferred_element_type=jnp.float32
    )
    centred = inner_prod - jnp.sum(softmax_rows * inner_prod, axis=-1, keepdims=True)
    score_grad = (softmax_rows * centred * score_scale).astype(jnp.bfloat16)
    query_part = jnp.einsum(
        "hrk,khd->rhd", score_grad, keys_head, preferred_element_type=jnp.float32
    )
    key_part = jnp.einsum("hrk,rhd->khd", score_grad, queries, preferred_element_type=jnp.float32)
    value_part = jnp.einsum(
        "hrk,rhd->khd", softmax_low, att_grad, preferred_element_type=jnp.float32
    )
    return (query_part, key_part, value_part)


def held_low(values):
    return lax.optimization_barrier(values.astype(jnp.bfloat16)).astype(jnp.float32)


def contract_rows(left, right):
    return lax.dot_general(
        left, right, (((0,), (0,)), ((), ())), preferred_element_type=jnp.float32
    )


def contract_cols(left, right):
    return lax.dot_general(
        left, right, (((1,), (1,)), ((), ())), preferred_element_type=jnp.float32
    )


def per_device(shallow, teacher, positions, segments, in_gain, w_query, w_keyval, w_output):
    group_rows = shallow.shape[0]
    pipe_count = lax.axis_size("pipe")
    data_count = lax.axis_size("dp")
    pipe_rank = lax.axis_index("pipe")
    block_rows = group_rows // pipe_count
    head_cols = w_query.shape[1]
    local_heads = head_cols // HD
    keyval_cols = w_keyval.shape[1]
    keyval_blocks = keyval_cols // HD
    all_rows = group_rows * data_count
    param_count = D * (2 * QH * HD + 2 * KV * HD)
    normed = normalize_rows(shallow, in_gain)
    cosine, sine_table = rotary_tables(positions, HD)
    columns = normed
    query_proj = jnp.dot(
        columns,
        lax.all_gather(w_query, "dp", axis=0, tiled=True),
        preferred_element_type=jnp.float32,
    )
    keyval_proj = jnp.dot(
        columns,
        lax.all_gather(w_keyval, "dp", axis=0, tiled=True),
        preferred_element_type=jnp.float32,
    )
    queries = rotate(query_proj.reshape(group_rows, local_heads, HD), cosine, sine_table).astype(
        jnp.bfloat16
    )
    keyval_local = keyval_proj.reshape(group_rows, keyval_blocks, HD)
    block_ids = pipe_rank * keyval_blocks + jnp.arange(keyval_blocks)
    is_key = (block_ids % 2 == 0)[None, :, None]
    keyval_local = jnp.where(is_key, rotate(keyval_local, cosine, sine_table), keyval_local).astype(
        jnp.bfloat16
    )
    keyval_all = lax.all_gather(
        keyval_local.reshape(group_rows, keyval_cols), "pipe", axis=1, tiled=True
    )
    keyval_all = keyval_all.reshape(group_rows, KV, 2, HD)
    head_ids = pipe_rank * local_heads + jnp.arange(local_heads)
    chooser = head_ids[:, None] % KV == jnp.arange(KV)[None, :]
    picked = jnp.einsum(
        "rksd,jk->rjsd",
        keyval_all,
        chooser.astype(jnp.bfloat16),
        preferred_element_type=jnp.float32,
    ).astype(jnp.bfloat16)
    keys_head = picked[:, :, 0]
    values_head = picked[:, :, 1]
    row_order = jnp.arange(group_rows)
    allowed = (segments[:, None] == segments[None, :]) & (row_order[None, :] <= row_order[:, None])
    softmax_rows, softmax_low, attended = attend(queries, keys_head, values_head, allowed)
    att_flat = attended.reshape(group_rows, head_cols)
    shallow_block = lax.dynamic_slice_in_dim(shallow, pipe_rank * block_rows, block_rows, 0)
    target = shifted(teacher, "pipe", 1).astype(jnp.float32)
    w_out_full = lax.all_gather(w_output, "dp", axis=1, tiled=True)
    partial_value = held_low(jnp.dot(att_flat, w_out_full, preferred_element_type=jnp.float32))
    out_rows = lax.psum_scatter(
        partial_value.astype(jnp.bfloat16), "pipe", scatter_dimension=0, tiled=True
    ).astype(jnp.float32)
    output = shallow_block.astype(jnp.float32) + out_rows
    norm_out = jnp.sqrt(jnp.sum(output * output, axis=-1, keepdims=True) + cosine_eps)
    norm_tar = jnp.sqrt(jnp.sum(target * target, axis=-1, keepdims=True) + cosine_eps)
    cosine_sim = jnp.sum(output * target, axis=-1, keepdims=True) / (norm_out * norm_tar)
    loss_local = jnp.sum(1.0 - cosine_sim)
    out_grad = (
        -(target / (norm_out * norm_tar) - cosine_sim * output / (norm_out * norm_out)) / all_rows
    ).astype(jnp.bfloat16)
    loss_total = lax.psum(loss_local, ("dp", "pipe"))
    grad_all = lax.all_gather(out_grad, "pipe", axis=0, tiled=True)
    att_grad = contract_cols(grad_all, w_out_full).astype(jnp.bfloat16)
    att_grad = att_grad.reshape(group_rows, local_heads, HD)
    query_part, key_part, value_part = attend_grad(
        softmax_rows, softmax_low, queries, keys_head, values_head, att_grad
    )
    query_grad = (
        unrotate(query_part, cosine, sine_table).astype(jnp.bfloat16).reshape(group_rows, head_cols)
    )
    spread_back = jnp.einsum(
        "rjsd,jk->rksd", jnp.stack([key_part, value_part], axis=2), chooser.astype(jnp.float32)
    )
    keyval_sum = lax.psum_scatter(
        spread_back.reshape(group_rows, 2 * KV * HD).astype(jnp.bfloat16),
        "pipe",
        scatter_dimension=1,
        tiled=True,
    ).astype(jnp.float32)
    keyval_sum = keyval_sum.reshape(group_rows, keyval_blocks, HD)
    keyval_grad = (
        jnp.where(is_key, unrotate(keyval_sum, cosine, sine_table), keyval_sum)
        .astype(jnp.bfloat16)
        .reshape(group_rows, keyval_cols)
    )
    grad_inputs = jnp.concatenate([query_grad, keyval_grad], axis=1)
    columns = normed
    grad_shard = lax.psum_scatter(
        jnp.concatenate(
            [contract_rows(columns, grad_inputs), contract_rows(grad_all, att_flat)], axis=1
        ).astype(jnp.bfloat16),
        "dp",
        scatter_dimension=0,
        tiled=True,
    ).astype(jnp.float32)
    grad_query = grad_shard[:, :head_cols]
    grad_keyval = grad_shard[:, head_cols : head_cols + keyval_cols]
    grad_output = grad_shard[:, head_cols + keyval_cols :].T
    squares = (
        jnp.sum(grad_query * grad_query)
        + jnp.sum(grad_keyval * grad_keyval)
        + jnp.sum(grad_output * grad_output)
    )
    square_total = lax.psum(squares, ("dp", "pipe"))
    grad_rms = jnp.sqrt(square_total / param_count + mean_eps)
    return (
        loss_total / all_rows,
        grad_query / grad_rms,
        grad_keyval / grad_rms,
        grad_output / grad_rms,
    )


def solution(mesh):
    placed = (
        P("dp", None),
        P(("dp", "pipe"), None),
        P("dp"),
        P("dp"),
        P(),
        P("dp", "pipe"),
        P("dp", "pipe"),
        P("pipe", "dp"),
    )
    return jax.shard_map(
        per_device,
        mesh=mesh,
        in_specs=placed,
        out_specs=(P(), P("dp", "pipe"), P("dp", "pipe"), P("pipe", "dp")),
        check_vma=False,
    )
```

profile of v0, /device:TPU:1, one launch (start us, length us, event | category | flops | bytes accessed | tf_op | source)
XLA Modules:
  0.0 725.1 jit_solution(165572289338817264)
XLA Ops:
  7.2 0.7 all-gather.5.cloned.1.call-update
  7.9 0.7 all-gather.7.cloned.1.call-update
  8.7 0.7 all-gather.9.cloned.1.call-update
  9.4 0.0 reduce-scatter.4.cloned.1.call-start
  9.4 0.7 convert_element_type.91
  10.2 3.1 fusion.2
  13.3 0.9 fusion.32
  14.1 0.5 multiply_cosine_fusion
  14.7 32.7 %all-gather.5.cloned.1.call-done = bf16[8192,128]{1,0:T(8,128)(2,1)} async-done(((bf16[512,128]{1,0:T(8,128)(2,1)}), bf16[8192,128]{1,0:T(8,128)(2,1)}) %all-gather.5.cloned.1.call-update) | async-done | bytes 2097168 | tf_op jit(solution)/shard_map/all_gather | solution.py:134
  47.4 4.6 fusion.72
  52.0 0.3 fusion.47
  52.4 29.5 %all_gather.16 = bf16[256,1024]{0,1:T(8,128)(2,1)S(1)} all-gather(bf16[256,128]{0,1:T(8,128)(2,1)S(1)} %fusion.37), channel_id=1, replica_groups=mesh['dp'=16,'pipe'=8] {'pipe'}, dimensions={1}, use_global_device_ids=true | all-gather | bytes 589824 | tf_op jit(solution)/shard_map/all_gather | solution.py:146
  81.8 0.3 copy.34
  82.2 0.5 fusion.13
  82.7 0.2 slice_bitcast_fusion
  82.9 0.2 copy.42
  83.0 26.8 %all-gather.7.cloned.1.call-done = bf16[8192,512]{1,0:T(8,128)(2,1)} async-done(((bf16[512,512]{1,0:T(8,128)(2,1)}), bf16[8192,512]{1,0:T(8,128)(2,1)}) %all-gather.7.cloned.1.call-update) | async-done | bytes 8388624 | tf_op jit(solution)/shard_map/all_gather | solution.py:129
  109.8 7.0 fusion.70
  116.8 0.2 reshape.251
  117.0 0.3 fusion.74
  117.4 0.1 subtract_convert_fusion.1
  117.5 0.6 fusion.75
  118.1 0.3 convolution_convert_fusion.5
  118.4 45.1 %all-gather.9.cloned.1.call-done = bf16[512,8192]{1,0:T(8,128)(2,1)} async-done(((bf16[512,512]{1,0:T(8,128)(2,1)}), bf16[512,8192]{1,0:T(8,128)(2,1)}) %all-gather.9.cloned.1.call-update) | async-done | bytes 8388624 | tf_op jit(solution)/shard_map/all_gather | solution.py:166
  163.5 7.8 %convolution_convert_fusion.2 = bf16[256,8192]{1,0:T(8,128)(2,1)} fusion(bf16[256,512]{0,1:T(8,128)(2,1)S(1)} %bitcast.64, bf16[512,8192]{1,0:T(8,128)(2,1)} %all-gather.9.cloned.1.call-done), kind=kOutput, calls=%fused_computation.7 | convolution fusion | flops 2149580800 | bytes 12845056 | tf_op jit(solution)/shard_map/dot_general | solution.py:167
  171.3 0.0 all-gather.11.cloned.1.call-start
  171.4 2.9 collective-permute-start
  174.3 15.5 %collective-permute-done = bf16[32,8192]{1,0:T(8,128)(2,1)S(1)} collective-permute-done((bf16[32,8192]{1,0:T(8,128)(2,1)S(1)}, bf16[32,8192]{1,0:T(8,128)(2,1)S(1)}, u32[]{:S(2)}, u32[]{:S(2)}) %collective-permute-start) | collective-permute-done | bytes 524320 | tf_op jit(solution)/shard_map/ppermute | solution.py:21
  189.8 69.8 %reduce-scatter.4.cloned.1.call-done = bf16[32,8192]{1,0:T(8,128)(2,1)} async-done(((bf16[256,8192]{1,0:T(8,128)(2,1)}), bf16[32,8192]{1,0:T(8,128)(2,1)}) %reduce-scatter.4.cloned.1.call-update) | async-done | bytes 524304 | tf_op jit(solution)/shard_map/reduce_scatter | solution.py:168
  259.6 1.7 multiply_reduce_fusion.2
  261.3 0.6 subtract_reduce_fusion
  261.9 2.4 fusion.19
  264.3 0.0 reduce-scatter.6.cloned.1.call-start
  264.4 71.0 %all-gather.11.cloned.1.call-done = bf16[256,8192]{1,0:T(8,128)(2,1)} async-done(((bf16[32,8192]{1,0:T(8,128)(2,1)}), bf16[256,8192]{1,0:T(8,128)(2,1)}) %all-gather.11.cloned.1.call-update) | async-done | bytes 4194320 | tf_op jit(solution)/shard_map/all_gather | solution.py:180
  335.3 7.0 convolution_convert_fusion.6
  342.4 0.1 copy.65
  342.5 0.3 convolution_bitcast_fusion
  342.8 0.3 fusion.34
  343.1 2.1 convolution_bitcast_fusion.1
  345.3 2.1 convolution_bitcast_fusion.2
  347.4 0.1 pad_maximum_fusion.1
  347.4 0.3 copy.50
  347.8 0.4 fusion.12
  348.2 1.1 copy.51
  349.3 0.0 reduce-scatter.8.cloned.1.call-start
  349.4 0.3 add_convert_fusion
  349.6 0.1 pad_maximum_fusion.3
  349.8 0.1 copy.45
  349.9 7.9 %convolution_convert_fusion.1 = bf16[8192,512]{0,1:T(8,128)(2,1)} fusion(bf16[256,512]{0,1:T(8,128)(2,1)S(1)} %bitcast.65, bf16[256,8192]{1,0:T(8,128)(2,1)} %all-gather.11.cloned.1.call-done), kind=kOutput, calls=%fused_computation.4 | convolution fusion | flops 2151677952 | bytes 12845056 | tf_op jit(solution)/shard_map/dot_general | solution.py:101
  357.8 58.6 %reduce-scatter.6.cloned.1.call-done = bf16[256,128]{0,1:T(8,128)(2,1)} async-done(((bf16[256,1024]{0,1:T(8,128)(2,1)}), bf16[256,128]{0,1:T(8,128)(2,1)}) %reduce-scatter.6.cloned.1.call-update) | async-done | bytes 65552 | tf_op jit(solution)/shard_map/reduce_scatter | solution.py:192
  416.5 0.8 convert_bitcast_fusion
  417.3 0.3 fusion.51
  417.6 0.9 fusion.36
  418.5 5.8 convolution_convert_fusion
  424.3 13.8 %pad_maximum_fusion = bf16[8192,1152]{0,1:T(8,128)(2,1)} fusion(bf16[8192,512]{0,1:T(8,128)(2,1)} %convolution_convert_fusion.1, bf16[8192,640]{0,1:T(8,128)(2,1)S(1)} %convolution_convert_fusion), kind=kLoop, calls=%fused_computation.2 | loop fusion | flops 37748736 | bytes 37748736 | tf_op jit(solution)/shard_map/concatenate | solution.py:207
  438.1 203.0 %reduce-scatter.8.cloned.1.call-done = bf16[512,1152]{0,1:T(8,128)(2,1)} async-done(((bf16[8192,1152]{0,1:T(8,128)(2,1)}), bf16[512,1152]{0,1:T(8,128)(2,1)}) %reduce-scatter.8.cloned.1.call-update) | async-done | bytes 1179664 | tf_op jit(solution)/shard_map/reduce_scatter | solution.py:206
  641.1 1.6 convert_element_type.111
  642.7 0.7 multiply_reduce_fusion.4
  643.4 0.9 multiply_reduce_fusion
  646.2 64.6 %all-reduce = (f32[]{:T(128)}, f32[]{:T(128)}) all-reduce(f32[]{:T(128)} %get-tuple-element.19, f32[]{:T(128)S(6)} %add.123), channel_id=1, replica_groups=mesh['dp'=16,'pipe'=8] {'dp','pipe'}, use_global_device_ids=true, to_apply=%region_8.9 | all-reduce | flops 2 | bytes 16 | tf_op jit(solution)/shard_map/psum | solution.py:179
  711.4 0.7 slice_divide_fusion.1
  712.2 1.2 divide_bitcast_fusion
  713.4 1.8 copy.53
  715.2 1.3 copy.52
  (19 shorter events, 0.2 us)
Async XLA Ops:
  7.2 40.2 %all-gather.5.cloned.1.call-start = ((), (), s32[]{:S(2)}) async-start(), calls=%async_computation.3 | async-start | bytes 2228224 | tf_op jit(solution)/shard_map/all_gather | solution.py:134
  7.9 101.9 %all-gather.7.cloned.1.call-start = ((), (), s32[]{:S(2)}) async-start(), calls=%async_computation.4 | async-start | bytes 8912896 | tf_op jit(solution)/shard_map/all_gather | solution.py:129
  8.6 154.9 %all-gather.9.cloned.1.call-start = ((), (), s32[]{:S(2)}) async-start(), calls=%async_computation.5 | async-start | bytes 8912896 | tf_op jit(solution)/shard_map/all_gather | solution.py:166
  9.4 250.3 %reduce-scatter.4.cloned.1.call-start = ((), (), s32[]{:S(2)}) async-start(), calls=%async_computation.6 | async-start | bytes 4718592 | tf_op jit(solution)/shard_map/reduce_scatter | solution.py:168
  10.1 99.7 %copy-start = (f32[8192]{0:T(1024)S(1)}, f32[8192]{0:T(1024)}, u32[]{:S(2)}) copy-start(f32[8192]{0:T(1024)} %param.12) | copy-start | bytes 98308
  118.1 45.4 %copy-start.2 = (f32[4,256,256]{1,2,0:T(8,128)}, f32[4,256,256]{1,2,0:T(8,128)S(1)}, u32[]{:S(2)}) copy-start(f32[4,256,256]{1,2,0:T(8,128)S(1)} %get-tuple-element.40) | copy-start | bytes 3145732
  163.5 7.9 %copy-start.1 = (bf16[32,8192]{1,0:T(8,128)(2,1)S(1)}, bf16[32,8192]{1,0:T(8,128)(2,1)}, u32[]{:S(2)}) copy-start(bf16[32,8192]{1,0:T(8,128)(2,1)} %param.9) | copy-start | bytes 1572868
  171.3 164.0 %all-gather.11.cloned.1.call-start = ((), (), s32[]{:S(2)}) async-start(), calls=%async_computation.7 | async-start | bytes 4718592 | tf_op jit(solution)/shard_map/all_gather | solution.py:180
  171.4 18.4 %collective-permute-start = (bf16[32,8192]{1,0:T(8,128)(2,1)S(1)}, bf16[32,8192]{1,0:T(8,128)(2,1)S(1)}, u32[]{:S(2)}, u32[]{:S(2)}) collective-permute-start(bf16[32,8192]{1,0:T(8,128)(2,1)S(1)} %copy-done.1), channel_id=1, source_target_pairs={{0,1},{1,2},{2,3},{3,4},{4,5},{5,6},{6,7},{7,0},{8,9},{9,10},{10,1... | collective-permute-start | bytes 1572872 | tf_op jit(solution)/shard_map/ppermute | solution.py:21
  264.3 78.2 %copy-start.3 = (f32[4,256,256]{1,2,0:T(8,128)S(1)}, f32[4,256,256]{1,2,0:T(8,128)}, u32[]{:S(2)}) copy-start(f32[4,256,256]{1,2,0:T(8,128)} %copy-done.2) | copy-start | bytes 3145732
  264.3 152.1 %reduce-scatter.6.cloned.1.call-start = ((), (), s32[]{:S(2)}) async-start(), calls=%async_computation.8 | async-start | bytes 589824 | tf_op jit(solution)/shard_map/reduce_scatter | solution.py:192
  349.3 291.8 %reduce-scatter.8.cloned.1.call-start = ((), (), s32[]{:S(2)}) async-start(), calls=%async_computation.9 | async-start | bytes 20054016 | tf_op jit(solution)/shard_map/reduce_scatter | solution.py:206
Sparse Core Ops, SparseCore 0:
  9.7 37.6 all-gather.4
  49.1 60.6 all-gather.6
  111.5 51.9 all-gather.8
  171.4 88.1 reduce-scatter.3
  264.4 70.8 all-gather.10
  349.4 66.9 reduce-scatter.5
  438.2 202.8 reduce-scatter.7
where the time goes:
time: 726 us; the launch traced here: 725 us
  waiting for transfers between devices  525 us (72%)
  blocking collectives  94 us (13%)
  matrix products  46.8 us (6%)
  other arithmetic  31.7 us (4%)
  between operations  18.8 us (3%)
    reduce_scatter x1, waiting for transfers between devices, per_device(): lax.psum_scatter(jnp.concatenate([contract_rows(columns, grad_inputs), co...  203 us
    all_gather x1, waiting for transfers between devices, per_device(): grad_all = lax.all_gather(out_grad, 'pipe', axis=0, tiled=True)  71 us
    reduce_scatter x1, waiting for transfers between devices, per_device(): lax.psum_scatter(partial_value.astype(jnp.bfloat16), 'pipe', scatter_dime...  69.8 us
    psum x1, blocking collectives, per_device(): loss_total = lax.psum(loss_local, ('dp', 'pipe'))  64.6 us
    reduce_scatter x1, waiting for transfers between devices, per_device(): lax.psum_scatter(spread_back.reshape(group_rows, 2 * KV * HD).astype(jnp....  58.6 us
    all_gather x1, waiting for transfers between devices, per_device(): w_out_full = lax.all_gather(w_output, 'dp', axis=1, tiled=True)  45.1 us
    all_gather x1, waiting for transfers between devices, per_device(): lax.all_gather(w_keyval, 'dp', axis=0, tiled=True)  32.7 us
    all_gather x1, blocking collectives, per_device(): lax.all_gather(keyval_local.reshape(group_rows, keyval_cols), 'pipe', axi...  29.5 us
  transfers between devices with their start and end apart: 8, of which 8 were waited for; matrix products, arithmetic and copies ran while one was open for 4% of the time, Pallas kernels for 0%

commit v1 on v0

--- a/solution.py
+++ b/solution.py
@@ -177,7 +177,9 @@
         -(target / (norm_out * norm_tar) - cosine_sim * output / (norm_out * norm_out)) / all_rows
     ).astype(jnp.bfloat16)
     loss_total = lax.psum(loss_local, ("dp", "pipe"))
-    grad_all = lax.all_gather(out_grad, "pipe", axis=0, tiled=True)
+    grad_all = jnp.concatenate(
+        lax.all_to_all(jnp.stack([out_grad] * lax.axis_size("pipe")), "pipe", 0, 0), axis=0
+    )
     att_grad = contract_cols(grad_all, w_out_full).astype(jnp.bfloat16)
     att_grad = att_grad.reshape(group_rows, local_heads, HD)
     query_part, key_part, value_part = attend_grad(

time: 726 us -> 708 us (0.975)
  waiting for transfers between devices: 525 us -> 457 us
  blocking collectives: 94 us -> 144 us
    all_gather x1 -> x0, waiting for transfers between devices: 71 us -> none  [per_device(): grad_all = lax.all_gather(out_grad, 'pipe', axis=0, tiled=True)]
    all_to_all x0 -> x1, blocking collectives: none -> 49.8 us  [per_device(): lax.all_to_all(jnp.stack([out_grad] * lax.axis_size('pipe')), 'pipe', 0, 0)]
  transfers between devices with their start and end apart: 8 -> 7, of which waited for: 8 -> 7; matrix products, arithmetic and copies ran while one was open for 4% -> 4% of each run, Pallas kernels for 0% -> 0%
where the time goes in v1:
time: 708 us
  waiting for transfers between devices  457 us (65%)
  blocking collectives  144 us (20%)
  matrix products  45.5 us (6%)
  other arithmetic  30.9 us (4%)
  between operations  18.8 us (3%)
  local copies, waits for them, and re-layouts  8.46 us (1%)
    reduce_scatter x1, waiting for transfers between devices, per_device(): lax.psum_scatter(jnp.concatenate([contract_rows(columns, grad_inputs), co...  203 us
    reduce_scatter x1, waiting for transfers between devices, per_device(): lax.psum_scatter(partial_value.astype(jnp.bfloat16), 'pipe', scatter_dime...  69.8 us
    psum x1, blocking collectives, per_device(): loss_total = lax.psum(loss_local, ('dp', 'pipe'))  64.7 us
    reduce_scatter x1, waiting for transfers between devices, per_device(): lax.psum_scatter(spread_back.reshape(group_rows, 2 * KV * HD).astype(jnp....  61.6 us
    all_to_all x1, blocking collectives, per_device(): lax.all_to_all(jnp.stack([out_grad] * lax.axis_size('pipe')), 'pipe', 0, 0)  49.8 us
    all_gather x1, waiting for transfers between devices, per_device(): w_out_full = lax.all_gather(w_output, 'dp', axis=1, tiled=True)  45.1 us
    all_gather x1, waiting for transfers between devices, per_device(): lax.all_gather(w_keyval, 'dp', axis=0, tiled=True)  32.7 us
    all_gather x1, blocking collectives, per_device(): lax.all_gather(keyval_local.reshape(group_rows, keyval_cols), 'pipe', axi...  29.5 us
  transfers between devices with their start and end apart: 7, of which 7 were waited for; matrix products, arithmetic and copies ran while one was open for 4% of the time, Pallas kernels for 0%

profile of v1, /device:TPU:1, one launch (start us, length us, event | category | flops | bytes accessed | tf_op | source)
XLA Modules:
  0.0 707.6 jit_solution(3399696065044364978)
XLA Ops:
  7.2 0.7 all-gather.4.cloned.1.call-update
  7.9 0.7 all-gather.6.cloned.1.call-update
  8.7 0.7 all-gather.8.cloned.1.call-update
  9.4 0.7 convert_element_type.91
  10.2 3.1 fusion.2
  13.3 0.9 fusion.32
  14.1 0.5 multiply_cosine_fusion
  14.7 32.7 %all-gather.4.cloned.1.call-done = bf16[8192,128]{1,0:T(8,128)(2,1)} async-done(((bf16[512,128]{1,0:T(8,128)(2,1)}), bf16[8192,128]{1,0:T(8,128)(2,1)}) %all-gather.4.cloned.1.call-update) | async-done | bytes 2097168 | tf_op jit(solution)/shard_map/all_gather | solution.py:134
  47.4 4.6 fusion.72
  52.0 0.3 fusion.47
  52.4 29.5 %all_gather.13 = bf16[256,1024]{0,1:T(8,128)(2,1)S(1)} all-gather(bf16[256,128]{0,1:T(8,128)(2,1)S(1)} %fusion.37), channel_id=1, replica_groups=mesh['dp'=16,'pipe'=8] {'pipe'}, dimensions={1}, use_global_device_ids=true | all-gather | bytes 589824 | tf_op jit(solution)/shard_map/all_gather | solution.py:146
  81.8 0.3 copy.34
  82.2 0.5 fusion.13
  82.7 0.2 slice_bitcast_fusion
  82.9 0.2 copy.42
  83.0 26.8 %all-gather.6.cloned.1.call-done = bf16[8192,512]{1,0:T(8,128)(2,1)} async-done(((bf16[512,512]{1,0:T(8,128)(2,1)}), bf16[8192,512]{1,0:T(8,128)(2,1)}) %all-gather.6.cloned.1.call-update) | async-done | bytes 8388624 | tf_op jit(solution)/shard_map/all_gather | solution.py:129
  109.8 7.0 fusion.70
  116.8 0.2 reshape.256
  117.0 0.3 fusion.74
  117.4 0.1 subtract_convert_fusion.1
  117.5 0.6 fusion.75
  118.1 0.3 convolution_convert_fusion.5
  118.4 45.1 %all-gather.8.cloned.1.call-done = bf16[512,8192]{1,0:T(8,128)(2,1)} async-done(((bf16[512,512]{1,0:T(8,128)(2,1)}), bf16[512,8192]{1,0:T(8,128)(2,1)}) %all-gather.8.cloned.1.call-update) | async-done | bytes 8388624 | tf_op jit(solution)/shard_map/all_gather | solution.py:166
  163.5 7.8 %convolution_convert_fusion.2 = bf16[256,8192]{1,0:T(8,128)(2,1)} fusion(bf16[256,512]{0,1:T(8,128)(2,1)S(1)} %bitcast.67, bf16[512,8192]{1,0:T(8,128)(2,1)} %all-gather.8.cloned.1.call-done), kind=kOutput, calls=%fused_computation.7 | convolution fusion | flops 2149580800 | bytes 12845056 | tf_op jit(solution)/shard_map/dot_general | solution.py:167
  171.3 0.0 reduce-scatter.6.cloned.1.call-start
  171.4 2.9 collective-permute-start
  174.3 15.5 %collective-permute-done = bf16[32,8192]{1,0:T(8,128)(2,1)S(1)} collective-permute-done((bf16[32,8192]{1,0:T(8,128)(2,1)S(1)}, bf16[32,8192]{1,0:T(8,128)(2,1)S(1)}, u32[]{:S(2)}, u32[]{:S(2)}) %collective-permute-start) | collective-permute-done | bytes 524320 | tf_op jit(solution)/shard_map/ppermute | solution.py:21
  189.8 69.8 %reduce-scatter.4.cloned.1.call-done = bf16[32,8192]{1,0:T(8,128)(2,1)} async-done(((bf16[256,8192]{1,0:T(8,128)(2,1)}), bf16[32,8192]{1,0:T(8,128)(2,1)}) %reduce-scatter.4.cloned.1.call-update) | async-done | bytes 524304 | tf_op jit(solution)/shard_map/reduce_scatter | solution.py:168
  259.6 1.7 multiply_reduce_fusion.2
  261.3 0.6 subtract_reduce_fusion
  261.9 1.6 fusion.19
  263.5 0.5 stack.8
  264.0 49.8 %all_to_all.5 = bf16[8,32,8192]{2,1,0:T(8,128)(2,1)S(1)} all-to-all(bf16[8,32,8192]{2,1,0:T(8,128)(2,1)S(1)} %stack.8), channel_id=1, replica_groups=mesh['dp'=16,'pipe'=8] {'pipe'}, dimensions={0} | all-to-all | bytes 8388608 | tf_op jit(solution)/shard_map/all_to_all | solution.py:181
  313.8 2.0 copy-done
  315.7 5.7 convolution_convert_fusion.6
  321.5 0.1 copy.65
  321.6 0.3 convolution_bitcast_fusion
  322.0 0.3 fusion.34
  322.2 2.1 convolution_bitcast_fusion.1
  324.4 2.1 convolution_bitcast_fusion.2
  326.5 0.1 pad_maximum_fusion.1
  326.5 0.3 copy.50
  326.9 0.4 fusion.12
  327.3 1.1 copy.51
  328.4 0.3 reduce-scatter.8.cloned.1.call-start
  328.7 0.3 add_convert_fusion
  329.0 0.1 pad_maximum_fusion.3
  329.1 0.1 copy.45
  329.3 7.9 %convolution_convert_fusion.1 = bf16[8192,512]{0,1:T(8,128)(2,1)} fusion(bf16[256,512]{0,1:T(8,128)(2,1)S(1)} %bitcast.68, bf16[256,8192]{1,0:T(8,128)(2,1)} %bitcast.63), kind=kOutput, calls=%fused_computation.4 | convolution fusion | flops 2151677952 | bytes 12845056 | tf_op jit(solution)/shard_map/dot_general | solution.py:101
  337.2 61.6 %reduce-scatter.6.cloned.1.call-done = bf16[256,128]{0,1:T(8,128)(2,1)} async-done(((bf16[256,1024]{0,1:T(8,128)(2,1)}), bf16[256,128]{0,1:T(8,128)(2,1)}) %reduce-scatter.6.cloned.1.call-update) | async-done | bytes 65552 | tf_op jit(solution)/shard_map/reduce_scatter | solution.py:194
  398.8 0.8 convert_bitcast_fusion
  399.7 0.3 fusion.51
  400.0 0.9 fusion.36
  400.8 5.8 convolution_convert_fusion
  406.6 13.8 %pad_maximum_fusion = bf16[8192,1152]{0,1:T(8,128)(2,1)} fusion(bf16[8192,512]{0,1:T(8,128)(2,1)} %convolution_convert_fusion.1, bf16[8192,640]{0,1:T(8,128)(2,1)S(1)} %convolution_convert_fusion), kind=kLoop, calls=%fused_computation.2 | loop fusion | flops 37748736 | bytes 37748736 | tf_op jit(solution)/shard_map/concatenate | solution.py:209
  420.5 203.0 %reduce-scatter.8.cloned.1.call-done = bf16[512,1152]{0,1:T(8,128)(2,1)} async-done(((bf16[8192,1152]{0,1:T(8,128)(2,1)}), bf16[512,1152]{0,1:T(8,128)(2,1)}) %reduce-scatter.8.cloned.1.call-update) | async-done | bytes 1179664 | tf_op jit(solution)/shard_map/reduce_scatter | solution.py:208
  623.5 1.6 convert_element_type.111
  625.1 0.7 multiply_reduce_fusion.4
  625.7 0.9 multiply_reduce_fusion
  628.6 64.7 %all-reduce = (f32[]{:T(128)}, f32[]{:T(128)}) all-reduce(f32[]{:T(128)} %get-tuple-element.19, f32[]{:T(128)S(6)} %add.123), channel_id=1, replica_groups=mesh['dp'=16,'pipe'=8] {'dp','pipe'}, use_global_device_ids=true, to_apply=%region_8.9 | all-reduce | flops 2 | bytes 16 | tf_op jit(solution)/shard_map/psum | solution.py:179
  694.0 0.7 slice_divide_fusion.1
  694.7 1.2 divide_bitcast_fusion
  695.9 1.8 copy.53
  697.7 1.3 copy.52
  (20 shorter events, 0.3 us)
Async XLA Ops:
  7.2 40.2 %all-gather.4.cloned.1.call-start = ((), (), s32[]{:S(2)}) async-start(), calls=%async_computation.4 | async-start | bytes 2228224 | tf_op jit(solution)/shard_map/all_gather | solution.py:134
  7.9 101.9 %all-gather.6.cloned.1.call-start = ((), (), s32[]{:S(2)}) async-start(), calls=%async_computation.5 | async-start | bytes 8912896 | tf_op jit(solution)/shard_map/all_gather | solution.py:129
  8.6 154.9 %all-gather.8.cloned.1.call-start = ((), (), s32[]{:S(2)}) async-start(), calls=%async_computation.6 | async-start | bytes 8912896 | tf_op jit(solution)/shard_map/all_gather | solution.py:166
  9.4 250.3 %reduce-scatter.4.cloned.1.call-start = ((), (), s32[]{:S(2)}) async-start(), calls=%async_computation.7 | async-start | bytes 4718592 | tf_op jit(solution)/shard_map/reduce_scatter | solution.py:168
  10.1 99.7 %copy-start.1 = (f32[8192]{0:T(1024)S(1)}, f32[8192]{0:T(1024)}, u32[]{:S(2)}) copy-start(f32[8192]{0:T(1024)} %param.12) | copy-start | bytes 98308
  118.1 45.4 %copy-start.3 = (f32[4,256,256]{1,2,0:T(8,128)}, f32[4,256,256]{1,2,0:T(8,128)S(1)}, u32[]{:S(2)}) copy-start(f32[4,256,256]{1,2,0:T(8,128)S(1)} %get-tuple-element.40) | copy-start | bytes 3145732
  163.5 7.9 %copy-start.2 = (bf16[32,8192]{1,0:T(8,128)(2,1)S(1)}, bf16[32,8192]{1,0:T(8,128)(2,1)}, u32[]{:S(2)}) copy-start(bf16[32,8192]{1,0:T(8,128)(2,1)} %param.9) | copy-start | bytes 1572868
  171.3 227.5 %reduce-scatter.6.cloned.1.call-start = ((), (), s32[]{:S(2)}) async-start(), calls=%async_computation.8 | async-start | bytes 589824 | tf_op jit(solution)/shard_map/reduce_scatter | solution.py:194
  171.4 18.4 %collective-permute-start = (bf16[32,8192]{1,0:T(8,128)(2,1)S(1)}, bf16[32,8192]{1,0:T(8,128)(2,1)S(1)}, u32[]{:S(2)}, u32[]{:S(2)}) collective-permute-start(bf16[32,8192]{1,0:T(8,128)(2,1)S(1)} %copy-done.2), channel_id=1, source_target_pairs={{0,1},{1,2},{2,3},{3,4},{4,5},{5,6},{6,7},{7,0},{8,9},{9,10},{10,1... | collective-permute-start | bytes 1572872 | tf_op jit(solution)/shard_map/ppermute | solution.py:21
  313.8 2.0 copy-start
  313.8 7.9 %copy-start.4 = (f32[4,256,256]{1,2,0:T(8,128)S(1)}, f32[4,256,256]{1,2,0:T(8,128)}, u32[]{:S(2)}) copy-start(f32[4,256,256]{1,2,0:T(8,128)} %copy-done.3) | copy-start | bytes 3145732
  328.4 295.0 %reduce-scatter.8.cloned.1.call-start = ((), (), s32[]{:S(2)}) async-start(), calls=%async_computation.9 | async-start | bytes 20054016 | tf_op jit(solution)/shard_map/reduce_scatter | solution.py:208
Sparse Core Ops, SparseCore 0:
  9.7 37.6 all-gather.3
  49.1 60.6 all-gather.5
  111.5 51.9 all-gather.7
  171.4 88.1 reduce-scatter.3
  328.6 70.1 reduce-scatter.5
  420.6 202.8 reduce-scatter.7
